TPU v7x, 32 devices: a whole 2x2x4 slice. The times are simulated.
32 devices in a mesh: parts: 2 (over y), row: 4 (over z), tile: 4 (over x, core).
Axes of the slice: x: 2, y: 2, z: 4, core: 2. Of those that a mesh axis runs over, the one named last changes fastest.
Arguments:
- mismatch: bfloat16 [8, 64, 4096], P(('parts', 'row'), None, 'tile'), parts along dimension 0, may hold values from -6 to 6
- col_weight: bfloat16 [4, 128, 128], P('row'), may hold values from -0.5 to 0.5
- row_weight: bfloat16 [14, 4, 64, 64], P(None, None, 'row'), may hold values from -0.75 to 0.75
- volume: float32 [4, 256, 2048], P('parts', 'row', 'tile'), parts along dimension 0, may hold values from -6 to 6
- step_size: float32 [4], P('parts'), parts along dimension 0, may hold values from 0.1 to 0.4
- combos: int32 [8, 4, 7, 16], P('parts'), parts along dimension 0, may hold values from 0 to 15, each once within a row
- dest_block: int32 [8, 4, 7, 16], P('parts'), parts along dimension 0, may hold values from 0 to 3
- counts: int32 [8, 4, 7, 4], P('parts'), parts along dimension 0, may hold values from 0 to 4, as said below
Outputs:
- volume_next: float32 [4, 256, 2048], P('parts', 'row', 'tile'), parts along dimension 0
There are 2 independent parts, one for each index of `parts`. A program takes and returns all parts, laid end to end along the dimension named above; an argument that names none is the same for every part. Nothing has to cross between parts.
Inputs may be any that keep to these rules, and one draw needn't show every extreme that they name: `combos`: for each source row group, tile group and offset, the last dimension is a permutation of 0 to 15. `counts`: zero where the destination row group g + j - 3 lies outside 0 to 3; at least 4 - abs(j - 3) elsewhere, except where that bound is below zero; in every draw some destination device receives 4 in every bucket from every valid source.
All inputs are finite; a program needn't handle non-finite values.
Results may differ from a plain program's by a relative error of at most 0.0031.
Values may be sent and summed in bfloat16 or wider, within the bound.
A program may use at most 64 MiB of HBM per device.

v0:
```python
import jax
import jax.numpy as jnp
from jax import lax
from jax.sharding import PartitionSpec as P


def shifted(shard, axis, by):
    length = lax.axis_size(axis)
    pairs = [(i, i + by) for i in range(length) if 0 <= i + by < length]
    return lax.ppermute(shard, axis, pairs)


def per_device(mismatch, col_weight, row_weight, volume, step_size, combos, dest_block, counts):
    ang_dev, det_rows, det_cols = mismatch.shape
    tile_edge = col_weight.shape[1]
    block_rows = row_weight.shape[3]
    col_blocks = det_cols // tile_edge
    depth_layers = volume.shape[0]
    voxel_blocks = volume.shape[2] // tile_edge
    band_width = row_weight.shape[0] // depth_layers
    reach_rows = band_width // 2
    tile_count = lax.axis_size("tile")
    row_count = lax.axis_size("row")
    slot_cap = combos.shape[3] // tile_count
    row_index = lax.axis_index("row")
    tile_index = lax.axis_index("tile")
    filtered = jnp.einsum(
        "arcv,avu->arcu",
        mismatch.reshape(ang_dev, det_rows, col_blocks, tile_edge),
        col_weight,
        preferred_element_type=jnp.float32,
    )
    filtered = filtered.astype(jnp.bfloat16).reshape(ang_dev, det_rows, det_cols)
    adjoint = jnp.einsum(
        "kary,arc->kyc",
        row_weight,
        lax.all_to_all(filtered, "row", split_axis=1, concat_axis=0, tiled=True),
        preferred_element_type=jnp.float32,
    ).astype(jnp.bfloat16)
    blocks_all = adjoint.reshape(band_width, depth_layers, block_rows, col_blocks, tile_edge)
    own_combo = combos[row_index, tile_index]
    offsets = jnp.arange(band_width, dtype=jnp.int32)[:, None]
    outgoing = blocks_all[offsets, own_combo // col_blocks, :, own_combo % col_blocks, :]
    outgoing = outgoing.reshape(band_width, tile_count, slot_cap, block_rows, tile_edge)
    pieces = [
        lax.all_to_all(
            shifted(outgoing[offset], "row", offset - reach_rows),
            "tile",
            split_axis=0,
            concat_axis=0,
            tiled=True,
        )
        for offset in range(band_width)
    ]
    incoming = jnp.stack(pieces)
    offset_ids = jnp.arange(band_width, dtype=jnp.int32)
    source_rows = row_index - (offset_ids - reach_rows)
    inside = (source_rows >= 0) & (source_rows < row_count)
    source_safe = jnp.clip(source_rows, 0, row_count - 1)
    tile_ids = jnp.arange(tile_count, dtype=jnp.int32)
    slot_ids = jnp.arange(slot_cap, dtype=jnp.int32)
    slot_cols = tile_index * slot_cap + slot_ids
    arriving = combos[
        source_safe[:, None, None],
        tile_ids[None, :, None],
        offset_ids[:, None, None],
        slot_cols[None, None, :],
    ]
    arriving_dest = dest_block[
        source_safe[:, None, None],
        tile_ids[None, :, None],
        offset_ids[:, None, None],
        slot_cols[None, None, :],
    ]
    arriving_count = counts[
        source_safe[:, None], tile_ids[None, :], offset_ids[:, None], tile_index
    ]
    live_slots = inside[:, None, None] & (slot_ids[None, None, :] < arriving_count[:, :, None])
    target = arriving // col_blocks * voxel_blocks + arriving_dest
    places = jnp.arange(depth_layers * voxel_blocks, dtype=jnp.int32)
    selector = ((target[..., None] == places) & live_slots[..., None]).astype(jnp.bfloat16)
    total_slots = band_width * tile_count * slot_cap
    selector = selector.reshape(total_slots, depth_layers, voxel_blocks)
    gradient = jnp.einsum(
        "szb,syx->zybx",
        selector,
        incoming.reshape(total_slots, block_rows, tile_edge),
        preferred_element_type=jnp.float32,
    )
    gradient = gradient.reshape(depth_layers, block_rows, voxel_blocks * tile_edge)
    return volume - step_size[:, None, None] * gradient


def solution(mesh):
    return jax.shard_map(
        per_device,
        mesh=mesh,
        in_specs=(
            P(("parts", "row"), None, "tile"),
            P("row", None, None),
            P(None, None, "row", None),
            P("parts", "row", "tile"),
            P("parts"),
            P("parts", None, None, None),
            P("parts", None, None, None),
            P("parts", None, None, None),
        ),
        out_specs=P("parts", "row", "tile"),
        check_vma=False,
    )
```

profile of v0, /device:TPU:1, one launch (start us, length us, event | category | flops | bytes accessed | tf_op | source)
XLA Modules:
  0.0 114.9 jit_solution(10115860489888155725)
XLA Ops:
  4.6 5.4 %all-to-all-start = ((bf16[4,2,8192]{2,1,0:T(2,128)(2,1)}), bf16[4,2,8192]{2,1,0:T(2,128)(2,1)S(1)}, u32[]{:S(2)}, u32[]{:S(2)}) async-start(bf16[4,2,8192]{2,1,0:T(2,128)(2,1)} %reshape.304), calls=%async_computation | async-start | bytes 262144 | tf_op jit(solution)/shard_map/all_to_all | solution.py:37
  10.4 4.5 %all-to-all-done = bf16[4,2,8192]{2,1,0:T(2,128)(2,1)S(1)} async-done(((bf16[4,2,8192]{2,1,0:T(2,128)(2,1)}), bf16[4,2,8192]{2,1,0:T(2,128)(2,1)S(1)}, u32[]{:S(2)}, u32[]{:S(2)}) %all-to-all-start) | async-done | bytes 131104 | tf_op jit(solution)/shard_map/all_to_all | solution.py:37
  16.3 1.8 %copy.31 = bf16[7,2,64,8,128]{4,2,3,1,0:T(8,128)(2,1)} copy(bf16[7,2,64,8,128]{4,3,2,1,0:T(8,128)(2,1)S(1)} %bitcast.75) | data formatting | bytes 3670016 | tf_op jit(solution)/shard_map/reshape | solution.py:40
  18.1 3.1 %gather_fusion = bf16[112,64,128]{2,1,0:T(8,128)(2,1)S(1)} fusion(bf16[7,2,64,8,128]{4,2,3,1,0:T(8,128)(2,1)} %copy.31, s32[112]{0:T(128)S(1)} %reshape.256), kind=kCustom, calls=%fused_computation | custom fusion | bytes 3671360 | tf_op jit(solution)/shard_map/gather | solution.py:43
  24.9 1.8 %gather_fusion.1 = s32[112]{0:T(128)S(1)} fusion(s32[4,4,7,16]{3,1,2,0:T(4,128)S(1)} %copy-done.1, s32[112]{0:T(128)S(1)} %reshape.262), kind=kCustom, calls=%fused_computation.1 | custom fusion | bytes 2688 | tf_op jit(solution)/shard_map/gather | solution.py:63
  26.8 1.8 %gather_fusion.2 = s32[112]{0:T(128)S(1)} fusion(s32[4,4,7,16]{3,1,2,0:T(4,128)S(1)} %copy-done.2, s32[112]{0:T(128)S(1)} %reshape.262), kind=kCustom, calls=%fused_computation.2 | custom fusion | bytes 2688 | tf_op jit(solution)/shard_map/gather | solution.py:69
  30.2 1.5 %collective-permute-done = bf16[4,4,64,128]{3,1,2,0:T(4,128)(2,1)} collective-permute-done((bf16[4,4,64,128]{3,1,2,0:T(4,128)(2,1)S(1)}, bf16[4,4,64,128]{3,1,2,0:T(4,128)(2,1)}, u32[]{:S(2)}, u32[]{:S(2)}) %collective-permute-start) | collective-permute-done | bytes 262176 | tf_op jit(solution)/shard_map/ppermute | solution.py:10
  31.7 6.5 %all-to-all-start.1 = ((bf16[4,4,64,128]{3,1,2,0:T(4,128)(2,1)}), bf16[4,4,64,128]{3,1,2,0:T(4,128)(2,1)S(1)}, u32[]{:S(2)}, u32[]{:S(2)}) async-start(bf16[4,4,64,128]{3,1,2,0:T(4,128)(2,1)} %collective-permute-done), calls=%async_computation.1 | async-start | bytes 524288 | tf_op jit(solution)/shard_map/all_to_all | solution.py:46
  41.4 2.9 %collective-permute-start.3 = (bf16[4,4,64,128]{3,1,2,0:T(4,128)(2,1)}, bf16[4,4,64,128]{3,1,2,0:T(4,128)(2,1)}, u32[]{:S(2)}, u32[]{:S(2)}) collective-permute-start(bf16[4,4,64,128]{3,1,2,0:T(4,128)(2,1)} %copy.35), channel_id=1, source_target_pairs={{0,0},{4,4},{8,8},{12,12},{1,1},{5,5},{9,9},{13,13},{2,2},{6,6},{1... | collective-permute-start | bytes 786440 | tf_op jit(solution)/shard_map/ppermute | solution.py:10
  44.5 4.7 %collective-permute-start.4 = (bf16[4,4,64,128]{3,1,2,0:T(4,128)(2,1)S(1)}, bf16[4,4,64,128]{3,1,2,0:T(4,128)(2,1)}, u32[]{:S(2)}, u32[]{:S(2)}) collective-permute-start(bf16[4,4,64,128]{3,1,2,0:T(4,128)(2,1)S(1)} %copy.36), channel_id=1, source_target_pairs={{0,4},{4,8},{8,12},{1,5},{5,9},{9,13},{2,6},{6,10},{10,14},{3,7},{... | collective-permute-start | bytes 786440 | tf_op jit(solution)/shard_map/ppermute | solution.py:10
  49.4 4.2 %collective-permute-start.5 = (bf16[4,4,64,128]{3,1,2,0:T(4,128)(2,1)S(1)}, bf16[4,4,64,128]{3,1,2,0:T(4,128)(2,1)}, u32[]{:S(2)}, u32[]{:S(2)}) collective-permute-start(bf16[4,4,64,128]{3,1,2,0:T(4,128)(2,1)S(1)} %copy.37), channel_id=1, source_target_pairs={{0,8},{4,12},{1,9},{5,13},{2,10},{6,14},{3,11},{7,15},{16,24},{20,... | collective-permute-start | bytes 786440 | tf_op jit(solution)/shard_map/ppermute | solution.py:10
  53.9 2.0 %collective-permute-start.6 = (bf16[4,4,64,128]{3,1,2,0:T(4,128)(2,1)S(1)}, bf16[4,4,64,128]{3,1,2,0:T(4,128)(2,1)}, u32[]{:S(2)}, u32[]{:S(2)}) collective-permute-start(bf16[4,4,64,128]{3,1,2,0:T(4,128)(2,1)S(1)} %copy.38), channel_id=1, source_target_pairs={{0,12},{1,13},{2,14},{3,15},{16,28},{17,29},{18,30},{19,31}} | collective-permute-start | bytes 786440 | tf_op jit(solution)/shard_map/ppermute | solution.py:10
  55.9 4.3 %all-to-all-start.2 = ((bf16[4,4,64,128]{3,1,2,0:T(4,128)(2,1)}), bf16[4,4,64,128]{3,1,2,0:T(4,128)(2,1)S(1)}, u32[]{:S(2)}, u32[]{:S(2)}) async-start(bf16[4,4,64,128]{3,1,2,0:T(4,128)(2,1)} %collective-permute-done.1), calls=%async_computation.2 | async-start | bytes 524288 | tf_op jit(solution)/shard_map/all_to_all | solution.py:46
  60.2 5.1 %all-to-all-done.2 = bf16[4,4,64,128]{3,1,2,0:T(4,128)(2,1)S(1)} async-done(((bf16[4,4,64,128]{3,1,2,0:T(4,128)(2,1)}), bf16[4,4,64,128]{3,1,2,0:T(4,128)(2,1)S(1)}, u32[]{:S(2)}, u32[]{:S(2)}) %all-to-all-start.2) | async-done | bytes 262176 | tf_op jit(solution)/shard_map/all_to_all | solution.py:46
  65.3 4.2 %all-to-all-start.3 = ((bf16[4,4,64,128]{3,1,2,0:T(4,128)(2,1)}), bf16[4,4,64,128]{3,1,2,0:T(4,128)(2,1)S(1)}, u32[]{:S(2)}, u32[]{:S(2)}) async-start(bf16[4,4,64,128]{3,1,2,0:T(4,128)(2,1)} %collective-permute-done.2), calls=%async_computation.3 | async-start | bytes 524288 | tf_op jit(solution)/shard_map/all_to_all | solution.py:46
  69.7 5.0 %all-to-all-done.3 = bf16[4,4,64,128]{3,1,2,0:T(4,128)(2,1)S(1)} async-done(((bf16[4,4,64,128]{3,1,2,0:T(4,128)(2,1)}), bf16[4,4,64,128]{3,1,2,0:T(4,128)(2,1)S(1)}, u32[]{:S(2)}, u32[]{:S(2)}) %all-to-all-start.3) | async-done | bytes 262176 | tf_op jit(solution)/shard_map/all_to_all | solution.py:46
  74.7 4.2 %all-to-all-start.4 = ((bf16[4,4,64,128]{3,1,2,0:T(4,128)(2,1)}), bf16[4,4,64,128]{3,1,2,0:T(4,128)(2,1)S(1)}, u32[]{:S(2)}, u32[]{:S(2)}) async-start(bf16[4,4,64,128]{3,1,2,0:T(4,128)(2,1)} %collective-permute-done.3), calls=%async_computation.4 | async-start | bytes 524288 | tf_op jit(solution)/shard_map/all_to_all | solution.py:46
  79.1 5.0 %all-to-all-done.4 = bf16[4,4,64,128]{3,1,2,0:T(4,128)(2,1)S(1)} async-done(((bf16[4,4,64,128]{3,1,2,0:T(4,128)(2,1)}), bf16[4,4,64,128]{3,1,2,0:T(4,128)(2,1)S(1)}, u32[]{:S(2)}, u32[]{:S(2)}) %all-to-all-start.4) | async-done | bytes 262176 | tf_op jit(solution)/shard_map/all_to_all | solution.py:46
  84.1 4.2 %all-to-all-start.5 = ((bf16[4,4,64,128]{3,1,2,0:T(4,128)(2,1)}), bf16[4,4,64,128]{3,1,2,0:T(4,128)(2,1)S(1)}, u32[]{:S(2)}, u32[]{:S(2)}) async-start(bf16[4,4,64,128]{3,1,2,0:T(4,128)(2,1)} %collective-permute-done.4), calls=%async_computation.5 | async-start | bytes 524288 | tf_op jit(solution)/shard_map/all_to_all | solution.py:46
  88.5 5.0 %all-to-all-done.5 = bf16[4,4,64,128]{3,1,2,0:T(4,128)(2,1)S(1)} async-done(((bf16[4,4,64,128]{3,1,2,0:T(4,128)(2,1)}), bf16[4,4,64,128]{3,1,2,0:T(4,128)(2,1)S(1)}, u32[]{:S(2)}, u32[]{:S(2)}) %all-to-all-start.5) | async-done | bytes 262176 | tf_op jit(solution)/shard_map/all_to_all | solution.py:46
  93.5 4.2 %all-to-all-start.6 = ((bf16[4,4,64,128]{3,1,2,0:T(4,128)(2,1)}), bf16[4,4,64,128]{3,1,2,0:T(4,128)(2,1)S(1)}, u32[]{:S(2)}, u32[]{:S(2)}) async-start(bf16[4,4,64,128]{3,1,2,0:T(4,128)(2,1)} %collective-permute-done.5), calls=%async_computation.6 | async-start | bytes 524288 | tf_op jit(solution)/shard_map/all_to_all | solution.py:46
  97.9 5.0 %all-to-all-done.6 = bf16[4,4,64,128]{3,1,2,0:T(4,128)(2,1)S(1)} async-done(((bf16[4,4,64,128]{3,1,2,0:T(4,128)(2,1)}), bf16[4,4,64,128]{3,1,2,0:T(4,128)(2,1)S(1)}, u32[]{:S(2)}, u32[]{:S(2)}) %all-to-all-start.6) | async-done | bytes 262176 | tf_op jit(solution)/shard_map/all_to_all | solution.py:46
  103.0 4.2 %all-to-all-start.7 = ((bf16[4,4,64,128]{3,1,2,0:T(4,128)(2,1)}), bf16[4,4,64,128]{3,1,2,0:T(4,128)(2,1)S(1)}, u32[]{:S(2)}, u32[]{:S(2)}) async-start(bf16[4,4,64,128]{3,1,2,0:T(4,128)(2,1)} %collective-permute-done.6), calls=%async_computation.7 | async-start | bytes 524288 | tf_op jit(solution)/shard_map/all_to_all | solution.py:46
  107.3 5.1 %all-to-all-done.7 = bf16[4,4,64,128]{3,1,2,0:T(4,128)(2,1)S(1)} async-done(((bf16[4,4,64,128]{3,1,2,0:T(4,128)(2,1)}), bf16[4,4,64,128]{3,1,2,0:T(4,128)(2,1)S(1)}, u32[]{:S(2)}, u32[]{:S(2)}) %all-to-all-start.7) | async-done | bytes 262176 | tf_op jit(solution)/shard_map/all_to_all | solution.py:46
  (68 shorter events, 18.6 us)
Async XLA Ops:
  0.0 15.0 %copy-start = (bf16[14,4,16,64]{3,2,1,0:T(8,128)(2,1)S(1)}, bf16[14,4,16,64]{3,2,1,0:T(8,128)(2,1)}, u32[]{:S(2)}) copy-start(bf16[14,4,16,64]{3,2,1,0:T(8,128)(2,1)} %param.10) | copy-start | bytes 344068
  0.0 10.1 %copy-start.1 = (s32[4,4,7,16]{3,1,2,0:T(4,128)S(1)}, s32[4,4,7,16]{3,1,2,0:T(4,128)}, u32[]{:S(2)}) copy-start(s32[4,4,7,16]{3,1,2,0:T(4,128)} %param.13) | copy-start | bytes 21508
  4.6 10.2 %all-to-all-start = ((bf16[4,2,8192]{2,1,0:T(2,128)(2,1)}), bf16[4,2,8192]{2,1,0:T(2,128)(2,1)S(1)}, u32[]{:S(2)}, u32[]{:S(2)}) async-start(bf16[4,2,8192]{2,1,0:T(2,128)(2,1)} %reshape.304), calls=%async_computation | async-start | bytes 262144 | tf_op jit(solution)/shard_map/all_to_all | solution.py:37
  21.1 2.5 %copy-start.3 = (s32[4,4,7,4]{2,3,1,0:T(4,128)S(1)}, s32[4,4,7,4]{2,3,1,0:T(4,128)}, u32[]{:S(2)}) copy-start(s32[4,4,7,4]{2,3,1,0:T(4,128)} %param.15) | copy-start | bytes 5380
  22.3 9.4 %collective-permute-start = (bf16[4,4,64,128]{3,1,2,0:T(4,128)(2,1)S(1)}, bf16[4,4,64,128]{3,1,2,0:T(4,128)(2,1)}, u32[]{:S(2)}, u32[]{:S(2)}) collective-permute-start(bf16[4,4,64,128]{3,1,2,0:T(4,128)(2,1)S(1)} %copy.32), channel_id=1, source_target_pairs={{12,0},{13,1},{14,2},{15,3},{28,16},{29,17},{30,18},{31,19}} | collective-permute-start | bytes 786440 | tf_op jit(solution)/shard_map/ppermute | solution.py:10
  24.9 1.8 %copy-start.2 = (s32[4,4,7,16]{3,1,2,0:T(4,128)S(1)}, s32[4,4,7,16]{3,1,2,0:T(4,128)}, u32[]{:S(2)}) copy-start(s32[4,4,7,16]{3,1,2,0:T(4,128)} %param.14) | copy-start | bytes 21508
  26.7 1.9 %copy-start.4 = (bf16[16,64,128]{2,1,0:T(8,128)(2,1)S(1)}, bf16[16,64,128]{2,1,0:T(8,128)(2,1)}, u32[]{:S(2)}) copy-start(bf16[16,64,128]{2,1,0:T(8,128)(2,1)} %get-tuple-element.10) | copy-start | bytes 786436
  28.9 24.9 %collective-permute-start.1 = (bf16[4,4,64,128]{3,1,2,0:T(4,128)(2,1)S(1)}, bf16[4,4,64,128]{3,1,2,0:T(4,128)(2,1)}, u32[]{:S(2)}, u32[]{:S(2)}) collective-permute-start(bf16[4,4,64,128]{3,1,2,0:T(4,128)(2,1)S(1)} %copy.33), channel_id=1, source_target_pairs={{8,0},{12,4},{9,1},{13,5},{10,2},{14,6},{11,3},{15,7},{24,16},{28,... | collective-permute-start | bytes 786440 | tf_op jit(solution)/shard_map/ppermute | solution.py:10
  31.7 24.2 %all-to-all-start.1 = ((bf16[4,4,64,128]{3,1,2,0:T(4,128)(2,1)}), bf16[4,4,64,128]{3,1,2,0:T(4,128)(2,1)S(1)}, u32[]{:S(2)}, u32[]{:S(2)}) async-start(bf16[4,4,64,128]{3,1,2,0:T(4,128)(2,1)} %collective-permute-done), calls=%async_computation.1 | async-start | bytes 524288 | tf_op jit(solution)/shard_map/all_to_all | solution.py:46
  39.1 21.1 %collective-permute-start.2 = (bf16[4,4,64,128]{3,1,2,0:T(4,128)(2,1)}, bf16[4,4,64,128]{3,1,2,0:T(4,128)(2,1)}, u32[]{:S(2)}, u32[]{:S(2)}) collective-permute-start(bf16[4,4,64,128]{3,1,2,0:T(4,128)(2,1)} %copy.34), channel_id=1, source_target_pairs={{4,0},{8,4},{12,8},{5,1},{9,5},{13,9},{6,2},{10,6},{14,10},{7,3},{... | collective-permute-start | bytes 786440 | tf_op jit(solution)/shard_map/ppermute | solution.py:10
  41.4 28.2 %collective-permute-start.3 = (bf16[4,4,64,128]{3,1,2,0:T(4,128)(2,1)}, bf16[4,4,64,128]{3,1,2,0:T(4,128)(2,1)}, u32[]{:S(2)}, u32[]{:S(2)}) collective-permute-start(bf16[4,4,64,128]{3,1,2,0:T(4,128)(2,1)} %copy.35), channel_id=1, source_target_pairs={{0,0},{4,4},{8,8},{12,12},{1,1},{5,5},{9,9},{13,13},{2,2},{6,6},{1... | collective-permute-start | bytes 786440 | tf_op jit(solution)/shard_map/ppermute | solution.py:10
  44.5 34.5 %collective-permute-start.4 = (bf16[4,4,64,128]{3,1,2,0:T(4,128)(2,1)S(1)}, bf16[4,4,64,128]{3,1,2,0:T(4,128)(2,1)}, u32[]{:S(2)}, u32[]{:S(2)}) collective-permute-start(bf16[4,4,64,128]{3,1,2,0:T(4,128)(2,1)S(1)} %copy.36), channel_id=1, source_target_pairs={{0,4},{4,8},{8,12},{1,5},{5,9},{9,13},{2,6},{6,10},{10,14},{3,7},{... | collective-permute-start | bytes 786440 | tf_op jit(solution)/shard_map/ppermute | solution.py:10
  49.4 39.0 %collective-permute-start.5 = (bf16[4,4,64,128]{3,1,2,0:T(4,128)(2,1)S(1)}, bf16[4,4,64,128]{3,1,2,0:T(4,128)(2,1)}, u32[]{:S(2)}, u32[]{:S(2)}) collective-permute-start(bf16[4,4,64,128]{3,1,2,0:T(4,128)(2,1)S(1)} %copy.37), channel_id=1, source_target_pairs={{0,8},{4,12},{1,9},{5,13},{2,10},{6,14},{3,11},{7,15},{16,24},{20,... | collective-permute-start | bytes 786440 | tf_op jit(solution)/shard_map/ppermute | solution.py:10
  53.9 44.0 %collective-permute-start.6 = (bf16[4,4,64,128]{3,1,2,0:T(4,128)(2,1)S(1)}, bf16[4,4,64,128]{3,1,2,0:T(4,128)(2,1)}, u32[]{:S(2)}, u32[]{:S(2)}) collective-permute-start(bf16[4,4,64,128]{3,1,2,0:T(4,128)(2,1)S(1)} %copy.38), channel_id=1, source_target_pairs={{0,12},{1,13},{2,14},{3,15},{16,28},{17,29},{18,30},{19,31}} | collective-permute-start | bytes 786440 | tf_op jit(solution)/shard_map/ppermute | solution.py:10
  55.9 9.4 %all-to-all-start.2 = ((bf16[4,4,64,128]{3,1,2,0:T(4,128)(2,1)}), bf16[4,4,64,128]{3,1,2,0:T(4,128)(2,1)S(1)}, u32[]{:S(2)}, u32[]{:S(2)}) async-start(bf16[4,4,64,128]{3,1,2,0:T(4,128)(2,1)} %collective-permute-done.1), calls=%async_computation.2 | async-start | bytes 524288 | tf_op jit(solution)/shard_map/all_to_all | solution.py:46
  65.3 9.4 %all-to-all-start.3 = ((bf16[4,4,64,128]{3,1,2,0:T(4,128)(2,1)}), bf16[4,4,64,128]{3,1,2,0:T(4,128)(2,1)S(1)}, u32[]{:S(2)}, u32[]{:S(2)}) async-start(bf16[4,4,64,128]{3,1,2,0:T(4,128)(2,1)} %collective-permute-done.2), calls=%async_computation.3 | async-start | bytes 524288 | tf_op jit(solution)/shard_map/all_to_all | solution.py:46
  74.7 9.4 %all-to-all-start.4 = ((bf16[4,4,64,128]{3,1,2,0:T(4,128)(2,1)}), bf16[4,4,64,128]{3,1,2,0:T(4,128)(2,1)S(1)}, u32[]{:S(2)}, u32[]{:S(2)}) async-start(bf16[4,4,64,128]{3,1,2,0:T(4,128)(2,1)} %collective-permute-done.3), calls=%async_computation.4 | async-start | bytes 524288 | tf_op jit(solution)/shard_map/all_to_all | solution.py:46
  84.1 9.4 %all-to-all-start.5 = ((bf16[4,4,64,128]{3,1,2,0:T(4,128)(2,1)}), bf16[4,4,64,128]{3,1,2,0:T(4,128)(2,1)S(1)}, u32[]{:S(2)}, u32[]{:S(2)}) async-start(bf16[4,4,64,128]{3,1,2,0:T(4,128)(2,1)} %collective-permute-done.4), calls=%async_computation.5 | async-start | bytes 524288 | tf_op jit(solution)/shard_map/all_to_all | solution.py:46
  93.5 9.4 %all-to-all-start.6 = ((bf16[4,4,64,128]{3,1,2,0:T(4,128)(2,1)}), bf16[4,4,64,128]{3,1,2,0:T(4,128)(2,1)S(1)}, u32[]{:S(2)}, u32[]{:S(2)}) async-start(bf16[4,4,64,128]{3,1,2,0:T(4,128)(2,1)} %collective-permute-done.5), calls=%async_computation.6 | async-start | bytes 524288 | tf_op jit(solution)/shard_map/all_to_all | solution.py:46
  103.0 9.4 %all-to-all-start.7 = ((bf16[4,4,64,128]{3,1,2,0:T(4,128)(2,1)}), bf16[4,4,64,128]{3,1,2,0:T(4,128)(2,1)S(1)}, u32[]{:S(2)}, u32[]{:S(2)}) async-start(bf16[4,4,64,128]{3,1,2,0:T(4,128)(2,1)} %collective-permute-done.6), calls=%async_computation.7 | async-start | bytes 524288 | tf_op jit(solution)/shard_map/all_to_all | solution.py:46
  113.1 1.0 copy-start.5
  113.1 0.9 copy-start.6
where the time goes:
time: 117 us; the launch traced here: 115 us
  starting transfers between devices  55.1 us (47%)
  waiting for transfers between devices  36.3 us (31%)
  local copies, waits for them, and re-layouts  18.7 us (16%)
  other arithmetic  2.55 us (2%)
  matrix products  2.02 us (2%)
    all_to_all x7, starting transfers between devices, per_device(): lax.all_to_all(shifted(outgoing[offset], 'row', offset - reach_rows), 'ti...  32 us
    all_to_all x7, waiting for transfers between devices, per_device(): lax.all_to_all(shifted(outgoing[offset], 'row', offset - reach_rows), 'ti...  30.3 us
    ppermute x7, starting transfers between devices, shifted(): return lax.ppermute(shard, axis, pairs)  17.7 us
    all_to_all x1, starting transfers between devices, per_device(): lax.all_to_all(filtered, 'row', split_axis=1, concat_axis=0, tiled=True)  5.42 us
    all_to_all x1, waiting for transfers between devices, per_device(): lax.all_to_all(filtered, 'row', split_axis=1, concat_axis=0, tiled=True)  4.47 us
    unnamed x26, local copies, waits for them, and re-layouts  3.94 us
    gather x1, local copies, waits for them, and re-layouts, per_device(): blocks_all[offsets, own_combo // col_blocks, :, own_combo % col_blocks, :]  3.06 us
    squeeze x7, local copies, waits for them, and re-layouts, per_device(): outgoing[offset]  2.85 us
  transfers between devices with their start and end apart: 15, of which 8 were waited for; matrix products, arithmetic and copies ran while one was open for 8% of the time, Pallas kernels for 0%

commit v1 on v0

--- a/solution.py
+++ b/solution.py
@@ -1,7 +1,209 @@
+import functools
+
 import jax
 import jax.numpy as jnp
 from jax import lax
+from jax.experimental import pallas as pl
+from jax.experimental.pallas import tpu as pltpu
 from jax.sharding import PartitionSpec as P
+
+MESH = pl.DeviceIdType.MESH
+
+
+def near_first(rows):
+    orders = [sorted(range(rows), key=lambda a: (abs(a - me), a)) for me in range(rows)]
+    return [sum(orders[me][k] * rows**me for me in range(rows)) for k in range(rows)]
+
+
+def kernel(
+    rows, tiles, reach, mis_ref, cw_ref, rw_ref, combos_ref, dest_ref, counts_ref, out_ref,
+    filt, work, weights, mask, picked, total, part_out, part_in,
+    w_send, w_recv, f_send, f_recv, p_send, p_recv, own_sem,
+):
+    me = lax.axis_index("row")
+    tile = lax.axis_index("tile")
+    edge = cw_ref.shape[0]
+    col_blocks = mis_ref.shape[1] // edge
+    depth = out_ref.shape[0]
+    group_rows = rw_ref.shape[2]
+    bx = out_ref.shape[2] // edge
+    cap = combos_ref.shape[3] // tiles
+
+    barrier = pltpu.get_barrier_semaphore()
+    for d in range(1, rows):
+        pl.semaphore_signal(barrier, inc=1, device_id={"row": lax.rem(me + d, rows)}, device_id_type=MESH)
+    for d in range(1, tiles):
+        pl.semaphore_signal(barrier, inc=1, device_id={"tile": lax.rem(tile + d, tiles)}, device_id_type=MESH)
+
+    for c in range(col_blocks):
+        filt[me, c] = jnp.dot(
+            mis_ref[:, c * edge:(c + 1) * edge], cw_ref[...], preferred_element_type=jnp.float32
+        ).astype(jnp.bfloat16)
+    own_w = pltpu.make_async_copy(rw_ref.at[pl.ds(depth * reach, depth)], weights.at[me], own_sem)
+    own_w.start()
+    pl.semaphore_wait(barrier, rows + tiles - 2)
+
+    codes = near_first(rows)
+    scale = jnp.int32(1)
+    for i in range(1, rows):
+        scale = scale * (1 + (rows - 1) * ((me + rows - i) // rows))
+    order = [(jnp.int32(code) // scale) % rows for code in codes]
+
+    w_copies, f_copies = [], []
+    for k in range(1, rows):
+        peer = order[k]
+        w_copies.append(pltpu.make_async_remote_copy(
+            src_ref=rw_ref.at[pl.ds(depth * (peer - me + reach), depth)],
+            dst_ref=weights.at[me],
+            send_sem=w_send.at[peer], recv_sem=w_recv.at[me],
+            device_id={"row": peer}, device_id_type=MESH,
+        ))
+        w_copies[-1].start()
+    for k in range(1, rows):
+        peer = order[k]
+        f_copies.append(pltpu.make_async_remote_copy(
+            src_ref=filt.at[me], dst_ref=filt.at[me],
+            send_sem=f_send.at[peer], recv_sem=f_recv.at[me],
+            device_id={"row": peer}, device_id_type=MESH,
+        ))
+        f_copies[-1].start()
+
+    def fill(i, carry):
+        g, q = i // (tiles * cap), i % (tiles * cap)
+        j = me - g + reach
+        m = combos_ref[g, tile, j, q]
+        place = (m // col_blocks) * bx + dest_ref[g, tile, j, q]
+        live = (q % cap) < counts_ref[g, tile, j, q // cap]
+        code = jnp.where(live, place, -1)
+        for n in range(depth * bx):
+            mask[i, n] = jnp.full(mask.shape[2:], jnp.where(code == n, 1.0, 0.0), jnp.float32).astype(jnp.bfloat16)
+        return carry
+
+    lax.fori_loop(0, rows * tiles * cap, fill, 0)
+
+    own_w.wait()
+    for k in range(1, rows):
+        src = order[k]
+        pltpu.make_async_remote_copy(
+            src_ref=rw_ref.at[pl.ds(0, depth)], dst_ref=weights.at[src],
+            send_sem=w_send.at[src], recv_sem=w_recv.at[src],
+            device_id={"row": src}, device_id_type=MESH,
+        ).wait_recv()
+
+    def term(a, t):
+        def group(g, carry):
+            at = pl.ds(pl.multiple_of(g * group_rows, group_rows), group_rows)
+            j = me - g + reach
+            slots = [(g * tiles + t) * cap + s for s in range(cap)]
+            blocks = [
+                work[combos_ref[g, tile, j, t * cap + s] % col_blocks, at, :] for s in range(cap)
+            ]
+            for n in range(depth * bx):
+                value = mask[slots[0], n] * blocks[0]
+                for s in range(1, cap):
+                    value = value + mask[slots[s], n] * blocks[s]
+                picked[n // bx, at, (n % bx) * edge:(n % bx + 1) * edge] = value
+            return carry
+
+        lax.fori_loop(0, rows, group, 0)
+        sums = []
+        for z in range(depth):
+            w = weights[:, z, pl.ds(a, 1), :, :].reshape(rows * group_rows, weights.shape[4])
+            sums.append(lax.dot_general(
+                w, picked[z], (((0,), (0,)), ((), ())), preferred_element_type=jnp.float32
+            ))
+        return sums
+
+    for k in range(rows - 1):
+        a = order[k]
+        if k:
+            pltpu.make_async_remote_copy(
+                src_ref=filt.at[a], dst_ref=filt.at[a],
+                send_sem=f_send.at[a], recv_sem=f_recv.at[a],
+                device_id={"row": a}, device_id_type=MESH,
+            ).wait_recv()
+
+        work[...] = filt[a]
+
+        def add(t, carry, a=a, k=k):
+            for z, s in enumerate(term(a, t)):
+                if k:
+                    total[t, z] += s
+                else:
+                    total[t, z] = s
+            return carry
+
+        lax.fori_loop(0, tiles, add, 0)
+
+    a = order[rows - 1]
+    pltpu.make_async_remote_copy(
+        src_ref=filt.at[a], dst_ref=filt.at[a],
+        send_sem=f_send.at[a], recv_sem=f_recv.at[a],
+        device_id={"row": a}, device_id_type=MESH,
+    ).wait_recv()
+    work[...] = filt[a]
+    pair = tile // 2
+    peers = []
+    for m in range(1, tiles // 2):
+        other = lax.rem(pair + m, tiles // 2)
+        peers += [other * 2 + tile % 2, other * 2 + 1 - tile % 2]
+    peers.append(pair * 2 + 1 - tile % 2)
+    p_copies = []
+    for t in peers:
+        for z, s in enumerate(term(a, t)):
+            part_out[t, z] = (total[t, z] + s).astype(jnp.bfloat16)
+        p_copies.append(pltpu.make_async_remote_copy(
+            src_ref=part_out.at[t], dst_ref=part_in.at[tile],
+            send_sem=p_send.at[t], recv_sem=p_recv.at[tile],
+            device_id={"tile": t}, device_id_type=MESH,
+        ))
+        p_copies[-1].start()
+    for z, s in enumerate(term(a, tile)):
+        out_ref[z] = total[tile, z] + s
+    for t in reversed(peers):
+        pltpu.make_async_remote_copy(
+            src_ref=part_out.at[t], dst_ref=part_in.at[t],
+            send_sem=p_send.at[t], recv_sem=p_recv.at[t],
+            device_id={"tile": t}, device_id_type=MESH,
+        ).wait_recv()
+        for z in range(depth):
+            out_ref[z] += part_in[t, z].astype(jnp.float32)
+    for copy in w_copies + f_copies + p_copies:
+        copy.wait_send()
+
+
+def gather_rows(rows, tiles, mismatch, col_weight, row_weight, volume, step_size, combos, dest_block, counts):
+    det_rows, det_cols = mismatch.shape[1:]
+    edge = col_weight.shape[1]
+    kinds, angles, group_rows, block_rows = row_weight.shape
+    depth = volume.shape[0]
+    reach = kinds // depth // 2
+    bx = volume.shape[2] // edge
+    cap = combos.shape[3] // tiles
+    bf16 = jnp.bfloat16
+    vmem, smem = pl.BlockSpec(memory_space=pltpu.VMEM), pl.BlockSpec(memory_space=pltpu.SMEM)
+    dma = pltpu.SemaphoreType.DMA
+    gradient = pl.pallas_call(
+        functools.partial(kernel, rows, tiles, reach),
+        out_shape=jax.ShapeDtypeStruct(volume.shape, jnp.float32),
+        in_specs=[vmem] * 3 + [smem] * 3,
+        out_specs=vmem,
+        scratch_shapes=[
+            pltpu.VMEM((rows, det_cols // edge, det_rows, edge), bf16),
+            pltpu.VMEM((det_cols // edge, det_rows, edge), bf16),
+            pltpu.VMEM((rows, depth, angles, group_rows, block_rows), bf16),
+            pltpu.VMEM((rows * tiles * cap, depth * bx, group_rows, edge), bf16),
+            pltpu.VMEM((depth, det_rows, bx * edge), bf16),
+            pltpu.VMEM((tiles,) + volume.shape, jnp.float32),
+            pltpu.VMEM((tiles,) + volume.shape, bf16),
+            pltpu.VMEM((tiles,) + volume.shape, bf16),
+            dma((rows,)), dma((rows,)), dma((rows,)), dma((rows,)), dma((tiles,)), dma((tiles,)), dma,
+        ],
+        compiler_params=pltpu.CompilerParams(
+            collective_id=0, has_side_effects=True, vmem_limit_bytes=32 * 2**20
+        ),
+    )(mismatch[0], col_weight[0], row_weight, combos, dest_block, counts)
+    return volume - step_size[:, None, None] * gradient
 
 
 def shifted(shard, axis, by):
@@ -92,8 +294,16 @@
 
 
 def solution(mesh):
+    rows, tiles = mesh.shape["row"], mesh.shape["tile"]
+
+    def body(mismatch, col_weight, row_weight, volume, *rest):
+        reach = row_weight.shape[0] // volume.shape[0] // 2
+        near = 1 < rows <= reach + 1 and tiles % 2 == 0 and mismatch.shape[0] == 1
+        run = functools.partial(gather_rows, rows, tiles) if near else per_device
+        return run(mismatch, col_weight, row_weight, volume, *rest)
+
     return jax.shard_map(
-        per_device,
+        body,
         mesh=mesh,
         in_specs=(
             P(("parts", "row"), None, "tile"),

time: 117 us -> 37.1 us (0.32); the launches traced: 115 us -> 36.8 us
  starting transfers between devices: 55.1 us -> 0 us
  waiting for transfers between devices: 36.3 us -> 0 us
  Pallas kernels: 0 us -> 32.4 us
  local copies, waits for them, and re-layouts: 18.7 us -> 3.57 us
  matrix products: 2.02 us -> 0 us
  other arithmetic: 2.55 us -> 0.8 us
    all_to_all x8 -> x0, starting transfers between devices: 37.4 us -> none  [the longest x7 32 us: per_device(): lax.all_to_all(shifted(outgoing[offset], 'row', offset - reach_rows), 'ti...]
    all_to_all x8 -> x0, waiting for transfers between devices: 34.8 us -> none  [the longest x7 30.3 us: per_device(): lax.all_to_all(shifted(outgoing[offset], 'row', offset - reach_rows), 'ti...]
    pallas_call x0 -> x1, Pallas kernels: none -> 32.4 us  [gather_rows(): pl.pallas_call(functools.partial(kernel, rows, tiles, reach), out_shape=j...]
    ppermute x7 -> x0, starting transfers between devices: 17.7 us -> none  [shifted(): return lax.ppermute(shard, axis, pairs)]
    gather x5 -> x0, local copies, waits for them, and re-layouts: 7.8 us -> none  [the longest x1 3.06 us: per_device(): blocks_all[offsets, own_combo // col_blocks, :, own_combo % col_blocks, :]]
    squeeze x7 -> x0, local copies, waits for them, and re-layouts: 2.85 us -> none  [per_device(): outgoing[offset]]
    reshape x3 -> x0, local copies, waits for them, and re-layouts: 2.04 us -> none  [the longest x1 1.79 us: per_device(): adjoint.reshape(band_width, depth_layers, block_rows, col_blocks, tile_edge)]
    dot_general x3 -> x0, matrix products: 2.02 us -> none  [the longest x1 0.93 us: per_device(): jnp.einsum('arcv,avu->arcu', mismatch.reshape(ang_dev, det_rows, col_bloc...]
  transfers between devices with their start and end apart: 15 -> 0, of which waited for: 8 -> 0; matrix products, arithmetic and copies ran while one was open for 8% -> 0% of each run, Pallas kernels for 0% -> 0%
where the time goes in v1:
time: 37.1 us; the launch traced here: 36.8 us
  Pallas kernels  32.4 us (87%)
  local copies, waits for them, and re-layouts  3.57 us (10%)
  other arithmetic  0.8 us (2%)
    pallas_call x1, Pallas kernels, gather_rows(): pl.pallas_call(functools.partial(kernel, rows, tiles, reach), out_shape=j...  32.4 us
    unnamed x13, local copies, waits for them, and re-layouts  3.57 us
    sub x1, other arithmetic, gather_rows(): return volume - step_size[:, None, None] * gradient  0.8 us

profile of v1, /device:TPU:1, one launch (start us, length us, event | category | flops | bytes accessed | tf_op | source)
XLA Modules:
  0.0 36.8 jit_solution(8855295901348682559)
XLA Ops:
  0.0 0.0 copy-start
  0.0 0.9 %copy.9.combos_ref = s32[4,4,7,16]{3,2,1,0:T(8,128)S(1)} copy(s32[4,4,7,16]{3,1,2,0:T(4,128)} %param.13) | data formatting | bytes 14336 | tf_op args[5]
  0.9 0.8 %copy.10.dest_ref = s32[4,4,7,16]{3,2,1,0:T(8,128)S(1)} copy(s32[4,4,7,16]{3,1,2,0:T(4,128)} %param.14) | data formatting | bytes 14336 | tf_op args[6]
  1.7 0.0 copy-start.2
  1.7 1.0 %copy.11.counts_ref = s32[4,4,7,4]{3,2,1,0:T(8,128)S(1)} copy(s32[4,4,7,4]{2,3,1,0:T(4,128)} %param.15) | data formatting | bytes 3584 | tf_op args[7]
  2.7 0.0 copy-done
  2.7 0.0 copy-done.2
  2.7 0.0 copy-start.1
  2.7 0.9 %copy-done.1 = bf16[1,64,1024]{2,1,0:T(8,128)(2,1)S(1)} copy-done((bf16[1,64,1024]{2,1,0:T(8,128)(2,1)S(1)}, bf16[1,64,1024]{2,1,0:T(8,128)(2,1)}, u32[]{:S(2)}) %copy-start.1) | copy-done | bytes 131096
  3.6 0.0 copy-start.3
  3.6 0.0 copy-start.4
  3.6 32.4 %shard_map.82 = f32[2,64,512]{2,1,0:T(8,128)S(1)} custom-call(bf16[64,1024]{1,0:T(8,128)(2,1)S(1)} %bitcast.2, bf16[128,128]{1,0:T(8,128)(2,1)S(1)} %bitcast.3, bf16[14,4,16,64]{3,2,1,0:T(8,128)(2,1)S(1)} %copy-done, s32[4,4,7,16]{3,2,1,0:T(8,128)S(1)} %copy.9.combos_ref, s32[4,4,7,16]{3,2,1,0:T(8,128)S(1)} %copy.10.dest_ref, s32[4,4,7,4]{3,2,1,0:T(8,128)S(1)} %copy.11.counts_ref), custom_call_target="tpu_custom_call" | custom-call | tf_op jit(solution)/shard_map/pallas_call | solution.py:186
  36.0 0.0 copy-done.3
  36.0 0.0 copy-done.4
  36.0 0.8 %multiply_subtract_fusion = f32[2,64,512]{2,1,0:T(8,128)} fusion(f32[2,64,512]{2,1,0:T(8,128)S(1)} %copy-done.3, f32[2,64,512]{2,1,0:T(8,128)S(1)} %shard_map.82, f32[2]{0:T(128)S(1)} %copy-done.4), kind=kLoop, calls=%fused_computation | loop fusion | flops 131072 | bytes 786440 | tf_op jit(solution)/shard_map/sub | solution.py:206
Async XLA Ops:
  0.0 2.7 %copy-start = (bf16[14,4,16,64]{3,2,1,0:T(8,128)(2,1)S(1)}, bf16[14,4,16,64]{3,2,1,0:T(8,128)(2,1)}, u32[]{:S(2)}) copy-start(bf16[14,4,16,64]{3,2,1,0:T(8,128)(2,1)} %rw_ref.1) | copy-start | bytes 344068
  1.7 1.0 %copy-start.2 = (bf16[1,128,128]{2,1,0:T(8,128)(2,1)S(1)}, bf16[1,128,128]{2,1,0:T(8,128)(2,1)}, u32[]{:S(2)}) copy-start(bf16[1,128,128]{2,1,0:T(8,128)(2,1)} %param.9) | copy-start | bytes 98308
  2.7 0.9 %copy-start.1 = (bf16[1,64,1024]{2,1,0:T(8,128)(2,1)S(1)}, bf16[1,64,1024]{2,1,0:T(8,128)(2,1)}, u32[]{:S(2)}) copy-start(bf16[1,64,1024]{2,1,0:T(8,128)(2,1)} %param.8) | copy-start | bytes 393220
  3.6 32.4 %copy-start.3 = (f32[2,64,512]{2,1,0:T(8,128)S(1)}, f32[2,64,512]{2,1,0:T(8,128)}, u32[]{:S(2)}) copy-start(f32[2,64,512]{2,1,0:T(8,128)} %param.11) | copy-start | bytes 786436
  3.6 32.4 %copy-start.4 = (f32[2]{0:T(128)S(1)}, f32[2]{0:T(128)}, u32[]{:S(2)}) copy-start(f32[2]{0:T(128)} %param.12) | copy-start | bytes 28

commit v2 on v1

--- a/solution.py
+++ b/solution.py
@@ -16,18 +16,21 @@
 
 
 def kernel(
-    rows, tiles, reach, mis_ref, cw_ref, rw_ref, combos_ref, dest_ref, counts_ref, out_ref,
-    filt, work, weights, mask, picked, total, part_out, part_in,
-    w_send, w_recv, f_send, f_recv, p_send, p_recv, own_sem,
+    rows, tiles, reach, mis_hbm, cw_hbm, rw_hbm, combos_hbm, dest_hbm, counts_hbm, out_ref,
+    mis_ref, cw_ref, rw_ref, combos_ref, dest_ref, counts_ref,
+    filt, work, packed, weights, mask, picked, total, part_out, part_in,
+    in_sem, rw_sem, int_sem, w_send, w_recv, f_send, f_recv, p_send, p_recv,
 ):
     me = lax.axis_index("row")
     tile = lax.axis_index("tile")
     edge = cw_ref.shape[0]
     col_blocks = mis_ref.shape[1] // edge
     depth = out_ref.shape[0]
-    group_rows = rw_ref.shape[2]
+    group_rows, block_rows = rw_ref.shape[3:]
     bx = out_ref.shape[2] // edge
-    cap = combos_ref.shape[3] // tiles
+    cap = combos_ref.shape[2] // tiles
+    halves = f_send.shape[2]
+    half = col_blocks // halves
 
     barrier = pltpu.get_barrier_semaphore()
     for d in range(1, rows):
@@ -35,13 +38,24 @@
     for d in range(1, tiles):
         pl.semaphore_signal(barrier, inc=1, device_id={"tile": lax.rem(tile + d, tiles)}, device_id_type=MESH)
 
-    for c in range(col_blocks):
-        filt[me, c] = jnp.dot(
-            mis_ref[:, c * edge:(c + 1) * edge], cw_ref[...], preferred_element_type=jnp.float32
-        ).astype(jnp.bfloat16)
-    own_w = pltpu.make_async_copy(rw_ref.at[pl.ds(depth * reach, depth)], weights.at[me], own_sem)
-    own_w.start()
-    pl.semaphore_wait(barrier, rows + tiles - 2)
+    loads = [
+        pltpu.make_async_copy(mis_hbm, mis_ref, in_sem.at[0]),
+        pltpu.make_async_copy(cw_hbm, cw_ref, in_sem.at[1]),
+    ]
+    w_loads = [
+        pltpu.make_async_copy(rw_hbm.at[pl.ds(depth * (r - me + reach), depth)], rw_ref.at[r], rw_sem.at[r])
+        for r in range(rows)
+    ]
+    int_loads = []
+    for g in range(rows):
+        j = me - g + reach
+        int_loads += [
+            pltpu.make_async_copy(combos_hbm.at[g, j], combos_ref.at[g], int_sem.at[0, g]),
+            pltpu.make_async_copy(dest_hbm.at[g, j], dest_ref.at[g], int_sem.at[1, g]),
+            pltpu.make_async_copy(counts_hbm.at[g, tile], counts_ref.at[g], int_sem.at[2, g]),
+        ]
+    for copy in loads + w_loads + int_loads:
+        copy.start()
 
     codes = near_first(rows)
     scale = jnp.int32(1)
@@ -49,31 +63,56 @@
         scale = scale * (1 + (rows - 1) * ((me + rows - i) // rows))
     order = [(jnp.int32(code) // scale) % rows for code in codes]
 
-    w_copies, f_copies = [], []
-    for k in range(1, rows):
+    for copy in loads:
+        copy.wait()
+    for c in range(col_blocks):
+        filt[me, c] = jnp.dot(
+            mis_ref[:, c * edge:(c + 1) * edge], cw_ref[...], preferred_element_type=jnp.float32
+        ).astype(jnp.bfloat16)
+    for r in range(rows):
+        w_loads[r].wait()
+        packed[r] = jnp.concatenate([rw_ref[r, z] for z in range(depth)], axis=-1)
+    weights[me] = packed[me]
+    pl.semaphore_wait(barrier, rows + tiles - 2)
+
+    def w_copy(k):
         peer = order[k]
-        w_copies.append(pltpu.make_async_remote_copy(
-            src_ref=rw_ref.at[pl.ds(depth * (peer - me + reach), depth)],
-            dst_ref=weights.at[me],
+        return pltpu.make_async_remote_copy(
+            src_ref=packed.at[peer], dst_ref=weights.at[me],
             send_sem=w_send.at[peer], recv_sem=w_recv.at[me],
             device_id={"row": peer}, device_id_type=MESH,
-        ))
-        w_copies[-1].start()
+        )
+
+    def f_copy(a, side, h):
+        return pltpu.make_async_remote_copy(
+            src_ref=filt.at[a, pl.ds(h * half, half)], dst_ref=filt.at[a, pl.ds(h * half, half)],
+            send_sem=f_send.at[a, side, h], recv_sem=f_recv.at[a, h],
+            device_id={"row": lax.rem(me + rows - 1 + 2 * side, rows)}, device_id_type=MESH,
+        )
+
+    def goes(a, side):
+        if side:
+            return jnp.logical_and(a <= me, me + 1 < rows)
+        return jnp.logical_and(a >= me, me > 0)
+
+    def forward(a, h):
+        for side in range(2):
+            @pl.when(goes(a, side))
+            def _():
+                f_copy(a, side, h).start()
+
     for k in range(1, rows):
-        peer = order[k]
-        f_copies.append(pltpu.make_async_remote_copy(
-            src_ref=filt.at[me], dst_ref=filt.at[me],
-            send_sem=f_send.at[peer], recv_sem=f_recv.at[me],
-            device_id={"row": peer}, device_id_type=MESH,
-        ))
-        f_copies[-1].start()
+        w_copy(k).start()
+    for h in range(halves):
+        forward(me, h)
+
+    for copy in int_loads:
+        copy.wait()
 
     def fill(i, carry):
         g, q = i // (tiles * cap), i % (tiles * cap)
-        j = me - g + reach
-        m = combos_ref[g, tile, j, q]
-        place = (m // col_blocks) * bx + dest_ref[g, tile, j, q]
-        live = (q % cap) < counts_ref[g, tile, j, q // cap]
+        place = (combos_ref[g, tile, q] // col_blocks) * bx + dest_ref[g, tile, q]
+        live = (q % cap) < counts_ref[g, q // cap, me - g + reach]
         code = jnp.where(live, place, -1)
         for n in range(depth * bx):
             mask[i, n] = jnp.full(mask.shape[2:], jnp.where(code == n, 1.0, 0.0), jnp.float32).astype(jnp.bfloat16)
@@ -81,11 +120,10 @@
 
     lax.fori_loop(0, rows * tiles * cap, fill, 0)
 
-    own_w.wait()
     for k in range(1, rows):
         src = order[k]
         pltpu.make_async_remote_copy(
-            src_ref=rw_ref.at[pl.ds(0, depth)], dst_ref=weights.at[src],
+            src_ref=packed.at[src], dst_ref=weights.at[src],
             send_sem=w_send.at[src], recv_sem=w_recv.at[src],
             device_id={"row": src}, device_id_type=MESH,
         ).wait_recv()
@@ -93,11 +131,8 @@
     def term(a, t):
         def group(g, carry):
             at = pl.ds(pl.multiple_of(g * group_rows, group_rows), group_rows)
-            j = me - g + reach
             slots = [(g * tiles + t) * cap + s for s in range(cap)]
-            blocks = [
-                work[combos_ref[g, tile, j, t * cap + s] % col_blocks, at, :] for s in range(cap)
-            ]
+            blocks = [work[combos_ref[g, tile, t * cap + s] % col_blocks, at, :] for s in range(cap)]
             for n in range(depth * bx):
                 value = mask[slots[0], n] * blocks[0]
                 for s in range(1, cap):
@@ -106,26 +141,20 @@
             return carry
 
         lax.fori_loop(0, rows, group, 0)
-        sums = []
-        for z in range(depth):
-            w = weights[:, z, pl.ds(a, 1), :, :].reshape(rows * group_rows, weights.shape[4])
-            sums.append(lax.dot_general(
-                w, picked[z], (((0,), (0,)), ((), ())), preferred_element_type=jnp.float32
-            ))
-        return sums
-
-    for k in range(rows - 1):
+        w = weights[:, pl.ds(a, 1), :, :].reshape(rows * group_rows, weights.shape[3])
+        return [
+            lax.dot_general(
+                w[:, z * block_rows:(z + 1) * block_rows], picked[z],
+                (((0,), (0,)), ((), ())), preferred_element_type=jnp.float32,
+            )
+            for z in range(depth)
+        ]
+
+    def accumulate(k):
         a = order[k]
-        if k:
-            pltpu.make_async_remote_copy(
-                src_ref=filt.at[a], dst_ref=filt.at[a],
-                send_sem=f_send.at[a], recv_sem=f_recv.at[a],
-                device_id={"row": a}, device_id_type=MESH,
-            ).wait_recv()
-
         work[...] = filt[a]
 
-        def add(t, carry, a=a, k=k):
+        def add(t, carry):
             for z, s in enumerate(term(a, t)):
                 if k:
                     total[t, z] += s
@@ -135,12 +164,23 @@
 
         lax.fori_loop(0, tiles, add, 0)
 
+    def arrive(k):
+        a = order[k]
+        for h in range(halves):
+            f_copy(a, 0, h).wait_recv()
+            forward(a, h)
+
+    accumulate(0)
+    waiting = []
+    for k in range(1, rows - 1):
+        arrive(k)
+        waiting.append(k)
+        if k % 2 == 0 or k == rows - 2:
+            for w in waiting:
+                accumulate(w)
+            waiting = []
+    arrive(rows - 1)
     a = order[rows - 1]
-    pltpu.make_async_remote_copy(
-        src_ref=filt.at[a], dst_ref=filt.at[a],
-        send_sem=f_send.at[a], recv_sem=f_recv.at[a],
-        device_id={"row": a}, device_id_type=MESH,
-    ).wait_recv()
     work[...] = filt[a]
     pair = tile // 2
     peers = []
@@ -168,7 +208,15 @@
         ).wait_recv()
         for z in range(depth):
             out_ref[z] += part_in[t, z].astype(jnp.float32)
-    for copy in w_copies + f_copies + p_copies:
+    for k in range(1, rows):
+        w_copy(k).wait_send()
+    for a in range(rows):
+        for side in range(2):
+            @pl.when(goes(a, side))
+            def _():
+                for h in range(halves):
+                    f_copy(a, side, h).wait_send()
+    for copy in p_copies:
         copy.wait_send()
 
 
@@ -177,32 +225,44 @@
     edge = col_weight.shape[1]
     kinds, angles, group_rows, block_rows = row_weight.shape
     depth = volume.shape[0]
-    reach = kinds // depth // 2
+    band = kinds // depth
     bx = volume.shape[2] // edge
     cap = combos.shape[3] // tiles
+    col_blocks = det_cols // edge
+    halves = 2 - col_blocks % 2
     bf16 = jnp.bfloat16
-    vmem, smem = pl.BlockSpec(memory_space=pltpu.VMEM), pl.BlockSpec(memory_space=pltpu.SMEM)
-    dma = pltpu.SemaphoreType.DMA
+    hbm, dma = pl.BlockSpec(memory_space=pltpu.HBM), pltpu.SemaphoreType.DMA
     gradient = pl.pallas_call(
-        functools.partial(kernel, rows, tiles, reach),
+        functools.partial(kernel, rows, tiles, band // 2),
         out_shape=jax.ShapeDtypeStruct(volume.shape, jnp.float32),
-        in_specs=[vmem] * 3 + [smem] * 3,
-        out_specs=vmem,
+        in_specs=[hbm] * 6,
+        out_specs=pl.BlockSpec(memory_space=pltpu.VMEM),
         scratch_shapes=[
-            pltpu.VMEM((rows, det_cols // edge, det_rows, edge), bf16),
-            pltpu.VMEM((det_cols // edge, det_rows, edge), bf16),
+            pltpu.VMEM((det_rows, det_cols), bf16),
+            pltpu.VMEM((edge, edge), bf16),
             pltpu.VMEM((rows, depth, angles, group_rows, block_rows), bf16),
+            pltpu.SMEM((rows, tiles, combos.shape[3]), jnp.int32),
+            pltpu.SMEM((rows, tiles, combos.shape[3]), jnp.int32),
+            pltpu.SMEM((rows, tiles, band), jnp.int32),
+            pltpu.VMEM((rows, col_blocks, det_rows, edge), bf16),
+            pltpu.VMEM((col_blocks, det_rows, edge), bf16),
+            pltpu.VMEM((rows, angles, group_rows, depth * block_rows), bf16),
+            pltpu.VMEM((rows, angles, group_rows, depth * block_rows), bf16),
             pltpu.VMEM((rows * tiles * cap, depth * bx, group_rows, edge), bf16),
             pltpu.VMEM((depth, det_rows, bx * edge), bf16),
             pltpu.VMEM((tiles,) + volume.shape, jnp.float32),
             pltpu.VMEM((tiles,) + volume.shape, bf16),
             pltpu.VMEM((tiles,) + volume.shape, bf16),
-            dma((rows,)), dma((rows,)), dma((rows,)), dma((rows,)), dma((tiles,)), dma((tiles,)), dma,
+            dma((2,)), dma((rows,)), dma((3, rows)), dma((rows,)), dma((rows,)),
+            dma((rows, 2, halves)), dma((rows, halves)), dma((tiles,)), dma((tiles,)),
         ],
         compiler_params=pltpu.CompilerParams(
-            collective_id=0, has_side_effects=True, vmem_limit_bytes=32 * 2**20
+            collective_id=0, has_side_effects=True, vmem_limit_bytes=63 * 2**20
         ),
-    )(mismatch[0], col_weight[0], row_weight, combos, dest_block, counts)
+    )(
+        mismatch[0], col_weight[0], row_weight,
+        combos.transpose(0, 2, 1, 3), dest_block.transpose(0, 2, 1, 3), counts.transpose(0, 1, 3, 2),
+    )
     return volume - step_size[:, None, None] * gradient
 
 

time: 37.1 us -> 26.6 us (0.72)
  Pallas kernels: 32.4 us -> 24.7 us
  local copies, waits for them, and re-layouts: 3.57 us -> 0.01 us
  other arithmetic: 0.8 us -> 1.75 us
    pallas_call x1, Pallas kernels: 32.4 us -> 24.7 us  [gather_rows(): pl.pallas_call(functools.partial(kernel, rows, tiles, band // 2), out_sha...]
    unnamed x13 -> x4, local copies, waits for them, and re-layouts: 3.57 us -> 0.01 us
    sub x1, other arithmetic: 0.8 us -> 1.75 us  [gather_rows(): return volume - step_size[:, None, None] * gradient]
where the time goes in v2:
time: 26.6 us; the launch traced here: 26.5 us
  Pallas kernels  24.7 us (93%)
  other arithmetic  1.75 us (7%)
    pallas_call x1, Pallas kernels, gather_rows(): pl.pallas_call(functools.partial(kernel, rows, tiles, band // 2), out_sha...  24.7 us
    sub x1, other arithmetic, gather_rows(): return volume - step_size[:, None, None] * gradient  1.75 us

profile of v2, /device:TPU:1, one launch (start us, length us, event | category | flops | bytes accessed | tf_op | source)
XLA Modules:
  0.0 26.5 jit_solution(17951119681353697628)
XLA Ops:
  0.0 0.0 copy-start
  0.0 0.0 copy-start.1
  0.0 24.7 %shard_map.82 = f32[2,64,512]{2,1,0:T(8,128)} custom-call(bf16[64,1024]{1,0:T(8,128)(2,1)} %bitcast.5, bf16[128,128]{1,0:T(8,128)(2,1)} %bitcast.8, bf16[14,4,16,64]{3,2,1,0:T(8,128)(2,1)} %rw_hbm.1, s32[4,7,4,16]{3,2,1,0:T(4,128)} %bitcast.6, s32[4,7,4,16]{3,2,1,0:T(4,128)} %bitcast.7, s32[4,4,4,7]{3,2,1,0:T(4,128)} %bitcast.9), custom_call_target="tpu_custom_call" | custom-call | tf_op jit(solution)/shard_map/pallas_call | solution.py:235
  24.7 0.0 copy-done
  24.7 0.0 copy-done.1
  24.7 1.8 %multiply_subtract_fusion = f32[2,64,512]{2,1,0:T(8,128)} fusion(f32[2,64,512]{2,1,0:T(8,128)S(1)} %copy-done, f32[2,64,512]{2,1,0:T(8,128)} %shard_map.82, f32[2]{0:T(128)S(1)} %copy-done.1), kind=kLoop, calls=%fused_computation | loop fusion | flops 131072 | bytes 786440 | tf_op jit(solution)/shard_map/sub | solution.py:266
Async XLA Ops:
  0.0 24.7 %copy-start = (f32[2,64,512]{2,1,0:T(8,128)S(1)}, f32[2,64,512]{2,1,0:T(8,128)}, u32[]{:S(2)}) copy-start(f32[2,64,512]{2,1,0:T(8,128)} %param.11) | copy-start | bytes 786436
  0.0 24.7 %copy-start.1 = (f32[2]{0:T(128)S(1)}, f32[2]{0:T(128)}, u32[]{:S(2)}) copy-start(f32[2]{0:T(128)} %param.12) | copy-start | bytes 28

commit v3 on v2

--- a/solution.py
+++ b/solution.py
@@ -16,10 +16,10 @@
 
 
 def kernel(
-    rows, tiles, reach, mis_hbm, cw_hbm, rw_hbm, combos_hbm, dest_hbm, counts_hbm, out_ref,
-    mis_ref, cw_ref, rw_ref, combos_ref, dest_ref, counts_ref,
-    filt, work, packed, weights, mask, picked, total, part_out, part_in,
-    in_sem, rw_sem, int_sem, w_send, w_recv, f_send, f_recv, p_send, p_recv,
+    rows, tiles, reach, mis_hbm, cw_hbm, rw_hbm, combos_hbm, dest_hbm, counts_hbm, vol_hbm, step_hbm, out_ref,
+    mis_ref, cw_ref, rw_ref, combos_ref, dest_ref, counts_ref, vol_ref, step_ref,
+    filt, work, packed, weights, mask, picked, total,
+    in_sem, rw_sem, int_sem, w_send, w_recv, z_send, x_send, s_send, f_recv,
 ):
     me = lax.axis_index("row")
     tile = lax.axis_index("tile")
@@ -29,14 +29,18 @@
     group_rows, block_rows = rw_ref.shape[3:]
     bx = out_ref.shape[2] // edge
     cap = combos_ref.shape[2] // tiles
-    halves = f_send.shape[2]
+    halves = f_recv.shape[2]
     half = col_blocks // halves
 
     barrier = pltpu.get_barrier_semaphore()
     for d in range(1, rows):
         pl.semaphore_signal(barrier, inc=1, device_id={"row": lax.rem(me + d, rows)}, device_id_type=MESH)
-    for d in range(1, tiles):
-        pl.semaphore_signal(barrier, inc=1, device_id={"tile": lax.rem(tile + d, tiles)}, device_id_type=MESH)
+    pairs = tiles // 2
+    core = tile % 2
+    sibling = tile + 1 - 2 * core
+    mirrors = [lax.rem(tile // 2 + m, pairs) * 2 + core for m in range(1, pairs)]
+    for t in [sibling] + mirrors:
+        pl.semaphore_signal(barrier, inc=1, device_id={"tile": t}, device_id_type=MESH)
 
     loads = [
         pltpu.make_async_copy(mis_hbm, mis_ref, in_sem.at[0]),
@@ -52,9 +56,13 @@
         int_loads += [
             pltpu.make_async_copy(combos_hbm.at[g, j], combos_ref.at[g], int_sem.at[0, g]),
             pltpu.make_async_copy(dest_hbm.at[g, j], dest_ref.at[g], int_sem.at[1, g]),
-            pltpu.make_async_copy(counts_hbm.at[g, tile], counts_ref.at[g], int_sem.at[2, g]),
+            pltpu.make_async_copy(counts_hbm.at[g], counts_ref.at[g], int_sem.at[2, g]),
         ]
-    for copy in loads + w_loads + int_loads:
+    late_loads = [
+        pltpu.make_async_copy(vol_hbm, vol_ref, in_sem.at[2]),
+        pltpu.make_async_copy(step_hbm, step_ref, in_sem.at[3]),
+    ]
+    for copy in loads + w_loads + int_loads + late_loads:
         copy.start()
 
     codes = near_first(rows)
@@ -66,14 +74,14 @@
     for copy in loads:
         copy.wait()
     for c in range(col_blocks):
-        filt[me, c] = jnp.dot(
+        filt[tile, me, c] = jnp.dot(
             mis_ref[:, c * edge:(c + 1) * edge], cw_ref[...], preferred_element_type=jnp.float32
         ).astype(jnp.bfloat16)
     for r in range(rows):
         w_loads[r].wait()
         packed[r] = jnp.concatenate([rw_ref[r, z] for z in range(depth)], axis=-1)
     weights[me] = packed[me]
-    pl.semaphore_wait(barrier, rows + tiles - 2)
+    pl.semaphore_wait(barrier, rows + pairs - 1)
 
     def w_copy(k):
         peer = order[k]
@@ -83,12 +91,24 @@
             device_id={"row": peer}, device_id_type=MESH,
         )
 
-    def f_copy(a, side, h):
+    def f_copy(t, a, h, sem, to):
+        piece = filt.at[t, a, pl.ds(h * half, half)]
         return pltpu.make_async_remote_copy(
-            src_ref=filt.at[a, pl.ds(h * half, half)], dst_ref=filt.at[a, pl.ds(h * half, half)],
-            send_sem=f_send.at[a, side, h], recv_sem=f_recv.at[a, h],
-            device_id={"row": lax.rem(me + rows - 1 + 2 * side, rows)}, device_id_type=MESH,
+            src_ref=piece, dst_ref=piece, send_sem=sem, recv_sem=f_recv.at[t, a, h],
+            device_id=to, device_id_type=MESH,
         )
+
+    def z_copy(a, side, h):
+        return f_copy(tile, a, h, z_send.at[a, side, h], {"row": lax.rem(me + rows - 1 + 2 * side, rows)})
+
+    def x_copies(a, h):
+        return [f_copy(tile, a, h, x_send.at[m, a, h], {"tile": t}) for m, t in enumerate(mirrors)]
+
+    def s_copy(t, a, h):
+        return f_copy(t, a, h, s_send.at[t, a, h], {"tile": sibling})
+
+    def wait_piece(t, a, h):
+        s_copy(t, a, h).wait_recv()
 
     def goes(a, side):
         if side:
@@ -99,20 +119,23 @@
         for side in range(2):
             @pl.when(goes(a, side))
             def _():
-                f_copy(a, side, h).start()
-
+                z_copy(a, side, h).start()
+
+        for copy in x_copies(a, h) + [s_copy(tile, a, h)]:
+            copy.start()
+
+    for h in range(halves):
+        forward(me, h)
     for k in range(1, rows):
         w_copy(k).start()
-    for h in range(halves):
-        forward(me, h)
 
     for copy in int_loads:
         copy.wait()
 
     def fill(i, carry):
-        g, q = i // (tiles * cap), i % (tiles * cap)
-        place = (combos_ref[g, tile, q] // col_blocks) * bx + dest_ref[g, tile, q]
-        live = (q % cap) < counts_ref[g, q // cap, me - g + reach]
+        g, t, s = i // (tiles * cap), i // cap % tiles, i % cap
+        place = (combos_ref[g, t, tile * cap + s] // col_blocks) * bx + dest_ref[g, t, tile * cap + s]
+        live = s < counts_ref[g, t, tile, me - g + reach]
         code = jnp.where(live, place, -1)
         for n in range(depth * bx):
             mask[i, n] = jnp.full(mask.shape[2:], jnp.where(code == n, 1.0, 0.0), jnp.float32).astype(jnp.bfloat16)
@@ -120,94 +143,76 @@
 
     lax.fori_loop(0, rows * tiles * cap, fill, 0)
 
-    for k in range(1, rows):
-        src = order[k]
-        pltpu.make_async_remote_copy(
-            src_ref=packed.at[src], dst_ref=weights.at[src],
-            send_sem=w_send.at[src], recv_sem=w_recv.at[src],
-            device_id={"row": src}, device_id_type=MESH,
-        ).wait_recv()
-
-    def term(a, t):
+    def weights_in():
+        for k in range(1, rows):
+            src = order[k]
+            pltpu.make_async_remote_copy(
+                src_ref=packed.at[src], dst_ref=weights.at[src],
+                send_sem=w_send.at[src], recv_sem=w_recv.at[src],
+                device_id={"row": src}, device_id_type=MESH,
+            ).wait_recv()
+
+    def accumulate(k):
+        a = order[k]
+        for t in range(tiles):
+            work[t] = filt[t, a]
+
         def group(g, carry):
             at = pl.ds(pl.multiple_of(g * group_rows, group_rows), group_rows)
-            slots = [(g * tiles + t) * cap + s for s in range(cap)]
-            blocks = [work[combos_ref[g, tile, t * cap + s] % col_blocks, at, :] for s in range(cap)]
+            sums = [None] * (depth * bx)
+            for t in range(tiles):
+                slots = [(g * tiles + t) * cap + s for s in range(cap)]
+                blocks = [
+                    work[t, combos_ref[g, t, tile * cap + s] % col_blocks, at, :] for s in range(cap)
+                ]
+                for n in range(depth * bx):
+                    value = mask[slots[0], n] * blocks[0]
+                    for s in range(1, cap):
+                        value = value + mask[slots[s], n] * blocks[s]
+                    value = value.astype(jnp.float32)
+                    sums[n] = value if t == 0 else sums[n] + value
             for n in range(depth * bx):
-                value = mask[slots[0], n] * blocks[0]
-                for s in range(1, cap):
-                    value = value + mask[slots[s], n] * blocks[s]
-                picked[n // bx, at, (n % bx) * edge:(n % bx + 1) * edge] = value
+                picked[n // bx, at, (n % bx) * edge:(n % bx + 1) * edge] = sums[n].astype(jnp.bfloat16)
             return carry
 
         lax.fori_loop(0, rows, group, 0)
         w = weights[:, pl.ds(a, 1), :, :].reshape(rows * group_rows, weights.shape[3])
-        return [
-            lax.dot_general(
+        for z in range(depth):
+            value = lax.dot_general(
                 w[:, z * block_rows:(z + 1) * block_rows], picked[z],
                 (((0,), (0,)), ((), ())), preferred_element_type=jnp.float32,
             )
-            for z in range(depth)
-        ]
-
-    def accumulate(k):
-        a = order[k]
-        work[...] = filt[a]
-
-        def add(t, carry):
-            for z, s in enumerate(term(a, t)):
+            if k:
+                value = total[z] + value
+            if k < rows - 1:
+                total[z] = value
+            else:
+                out_ref[z] = vol_ref[z] - step_ref[z] * value
+
+    for k in range(1, rows):
+        for h in range(halves):
+            wait_piece(tile, order[k], h)
+            forward(order[k], h)
+    for k in range(rows):
+        for h in range(halves):
+            for t in mirrors:
+                wait_piece(t, order[k], h)
+                s_copy(t, order[k], h).start()
+        if k == rows - 1:
+            for copy in late_loads:
+                copy.wait()
+        for p in range(pairs):
+            for h in range(halves):
                 if k:
-                    total[t, z] += s
-                else:
-                    total[t, z] = s
-            return carry
-
-        lax.fori_loop(0, tiles, add, 0)
-
-    def arrive(k):
-        a = order[k]
+                    wait_piece(p * 2 + 1 - core, order[k - 1], h)
+        if k == 1:
+            weights_in()
+        if k:
+            accumulate(k - 1)
+    for p in range(pairs):
         for h in range(halves):
-            f_copy(a, 0, h).wait_recv()
-            forward(a, h)
-
-    accumulate(0)
-    waiting = []
-    for k in range(1, rows - 1):
-        arrive(k)
-        waiting.append(k)
-        if k % 2 == 0 or k == rows - 2:
-            for w in waiting:
-                accumulate(w)
-            waiting = []
-    arrive(rows - 1)
-    a = order[rows - 1]
-    work[...] = filt[a]
-    pair = tile // 2
-    peers = []
-    for m in range(1, tiles // 2):
-        other = lax.rem(pair + m, tiles // 2)
-        peers += [other * 2 + tile % 2, other * 2 + 1 - tile % 2]
-    peers.append(pair * 2 + 1 - tile % 2)
-    p_copies = []
-    for t in peers:
-        for z, s in enumerate(term(a, t)):
-            part_out[t, z] = (total[t, z] + s).astype(jnp.bfloat16)
-        p_copies.append(pltpu.make_async_remote_copy(
-            src_ref=part_out.at[t], dst_ref=part_in.at[tile],
-            send_sem=p_send.at[t], recv_sem=p_recv.at[tile],
-            device_id={"tile": t}, device_id_type=MESH,
-        ))
-        p_copies[-1].start()
-    for z, s in enumerate(term(a, tile)):
-        out_ref[z] = total[tile, z] + s
-    for t in reversed(peers):
-        pltpu.make_async_remote_copy(
-            src_ref=part_out.at[t], dst_ref=part_in.at[t],
-            send_sem=p_send.at[t], recv_sem=p_recv.at[t],
-            device_id={"tile": t}, device_id_type=MESH,
-        ).wait_recv()
-        for z in range(depth):
-            out_ref[z] += part_in[t, z].astype(jnp.float32)
+            wait_piece(p * 2 + 1 - core, order[rows - 1], h)
+    accumulate(rows - 1)
     for k in range(1, rows):
         w_copy(k).wait_send()
     for a in range(rows):
@@ -215,9 +220,12 @@
             @pl.when(goes(a, side))
             def _():
                 for h in range(halves):
-                    f_copy(a, side, h).wait_send()
-    for copy in p_copies:
-        copy.wait_send()
+                    z_copy(a, side, h).wait_send()
+        for h in range(halves):
+            for copy in x_copies(a, h):
+                copy.wait_send()
+            for t in [tile] + mirrors:
+                s_copy(t, a, h).wait_send()
 
 
 def gather_rows(rows, tiles, mismatch, col_weight, row_weight, volume, step_size, combos, dest_block, counts):
@@ -232,10 +240,10 @@
     halves = 2 - col_blocks % 2
     bf16 = jnp.bfloat16
     hbm, dma = pl.BlockSpec(memory_space=pltpu.HBM), pltpu.SemaphoreType.DMA
-    gradient = pl.pallas_call(
+    return pl.pallas_call(
         functools.partial(kernel, rows, tiles, band // 2),
         out_shape=jax.ShapeDtypeStruct(volume.shape, jnp.float32),
-        in_specs=[hbm] * 6,
+        in_specs=[hbm] * 8,
         out_specs=pl.BlockSpec(memory_space=pltpu.VMEM),
         scratch_shapes=[
             pltpu.VMEM((det_rows, det_cols), bf16),
@@ -243,18 +251,19 @@
             pltpu.VMEM((rows, depth, angles, group_rows, block_rows), bf16),
             pltpu.SMEM((rows, tiles, combos.shape[3]), jnp.int32),
             pltpu.SMEM((rows, tiles, combos.shape[3]), jnp.int32),
-            pltpu.SMEM((rows, tiles, band), jnp.int32),
-            pltpu.VMEM((rows, col_blocks, det_rows, edge), bf16),
-            pltpu.VMEM((col_blocks, det_rows, edge), bf16),
+            pltpu.SMEM((rows, tiles, tiles, band), jnp.int32),
+            pltpu.VMEM(volume.shape, jnp.float32),
+            pltpu.SMEM(step_size.shape, jnp.float32),
+            pltpu.VMEM((tiles, rows, col_blocks, det_rows, edge), bf16),
+            pltpu.VMEM((tiles, col_blocks, det_rows, edge), bf16),
             pltpu.VMEM((rows, angles, group_rows, depth * block_rows), bf16),
             pltpu.VMEM((rows, angles, group_rows, depth * block_rows), bf16),
             pltpu.VMEM((rows * tiles * cap, depth * bx, group_rows, edge), bf16),
             pltpu.VMEM((depth, det_rows, bx * edge), bf16),
-            pltpu.VMEM((tiles,) + volume.shape, jnp.float32),
-            pltpu.VMEM((tiles,) + volume.shape, bf16),
-            pltpu.VMEM((tiles,) + volume.shape, bf16),
-            dma((2,)), dma((rows,)), dma((3, rows)), dma((rows,)), dma((rows,)),
-            dma((rows, 2, halves)), dma((rows, halves)), dma((tiles,)), dma((tiles,)),
+            pltpu.VMEM(volume.shape, jnp.float32),
+            dma((4,)), dma((rows,)), dma((3, rows)), dma((rows,)), dma((rows,)),
+            dma((rows, 2, halves)), dma((tiles // 2, rows, halves)), dma((tiles, rows, halves)),
+            dma((tiles, rows, halves)),
         ],
         compiler_params=pltpu.CompilerParams(
             collective_id=0, has_side_effects=True, vmem_limit_bytes=63 * 2**20
@@ -262,8 +271,8 @@
     )(
         mismatch[0], col_weight[0], row_weight,
         combos.transpose(0, 2, 1, 3), dest_block.transpose(0, 2, 1, 3), counts.transpose(0, 1, 3, 2),
+        volume, step_size,
     )
-    return volume - step_size[:, None, None] * gradient
 
 
 def shifted(shard, axis, by):

time: 26.6 us -> 25.8 us (0.970)
  other arithmetic: 1.75 us -> 0 us
  local copies, waits for them, and re-layouts: 0.01 us -> 1.67 us
  Pallas kernels: 24.7 us -> 23.9 us
    sub x1 -> x0, other arithmetic: 1.75 us -> none  [gather_rows(): return volume - step_size[:, None, None] * gradient]
    unnamed x4 -> x1, local copies, waits for them, and re-layouts: 0.01 us -> 1.67 us
    pallas_call x1, Pallas kernels: 24.7 us -> 23.9 us  [gather_rows(): pl.pallas_call(functools.partial(kernel, rows, tiles, band // 2), out_sha...]
where the time goes in v3:
time: 25.8 us; the launch traced here: 25.6 us
  Pallas kernels  23.9 us (93%)
  local copies, waits for them, and re-layouts  1.67 us (6%)
    pallas_call x1, Pallas kernels, gather_rows(): pl.pallas_call(functools.partial(kernel, rows, tiles, band // 2), out_sha...  23.9 us
    unnamed x1, local copies, waits for them, and re-layouts  1.67 us

profile of v3, /device:TPU:1, one launch (start us, length us, event | category | flops | bytes accessed | tf_op | source)
XLA Modules:
  0.0 25.6 jit_solution(1446414524608759914)
XLA Ops:
  0.0 23.9 %shard_map.82 = f32[2,64,512]{2,1,0:T(8,128)} custom-call(bf16[64,1024]{1,0:T(8,128)(2,1)} %bitcast.5, bf16[128,128]{1,0:T(8,128)(2,1)} %bitcast.8, bf16[14,4,16,64]{3,2,1,0:T(8,128)(2,1)} %rw_hbm.1, s32[4,7,4,16]{3,2,1,0:T(4,128)} %bitcast.6, s32[4,7,4,16]{3,2,1,0:T(4,128)} %bitcast.7, s32[4,4,4,7]{3,2,1,0:T(4,128)} %bitcast.9, f32[2,64,512]{2,1,0:T(8,128)} %vol_hbm.1, ...), custom_call_target="tpu_custom_call" | custom-call | tf_op jit(solution)/shard_map/pallas_call | solution.py:243
  23.9 1.7 %copy.10 = f32[2,64,512]{2,1,0:T(8,128)} copy(f32[2,64,512]{2,1,0:T(8,128)} %shard_map.82) | data formatting | bytes 524288

commit v4 on v3

--- a/solution.py
+++ b/solution.py
@@ -77,10 +77,6 @@
         filt[tile, me, c] = jnp.dot(
             mis_ref[:, c * edge:(c + 1) * edge], cw_ref[...], preferred_element_type=jnp.float32
         ).astype(jnp.bfloat16)
-    for r in range(rows):
-        w_loads[r].wait()
-        packed[r] = jnp.concatenate([rw_ref[r, z] for z in range(depth)], axis=-1)
-    weights[me] = packed[me]
     pl.semaphore_wait(barrier, rows + pairs - 1)
 
     def w_copy(k):
@@ -126,6 +122,10 @@
 
     for h in range(halves):
         forward(me, h)
+    for r in range(rows):
+        w_loads[r].wait()
+        packed[r] = jnp.concatenate([rw_ref[r, z] for z in range(depth)], axis=-1)
+    weights[me] = packed[me]
     for k in range(1, rows):
         w_copy(k).start()
 
@@ -266,13 +266,13 @@
             dma((tiles, rows, halves)),
         ],
         compiler_params=pltpu.CompilerParams(
-            collective_id=0, has_side_effects=True, vmem_limit_bytes=63 * 2**20
+            collective_id=0, has_side_effects=True, vmem_limit_bytes=32 * 2**20
         ),
-    )(
+    )(*(pltpu.with_memory_space_constraint(x, pltpu.HBM) for x in (
         mismatch[0], col_weight[0], row_weight,
         combos.transpose(0, 2, 1, 3), dest_block.transpose(0, 2, 1, 3), counts.transpose(0, 1, 3, 2),
         volume, step_size,
-    )
+    )))
 
 
 def shifted(shard, axis, by):

time: 25.8 us -> 24.1 us (0.934)
  local copies, waits for them, and re-layouts: 1.67 us -> 0.71 us
  Pallas kernels: 23.9 us -> 23.2 us
    unnamed x1, local copies, waits for them, and re-layouts: 1.67 us -> 0.71 us
    pallas_call x1, Pallas kernels: 23.9 us -> 23.2 us  [gather_rows(): pl.pallas_call(functools.partial(kernel, rows, tiles, band // 2), out_sha...]
where the time goes in v4:
time: 24.1 us; the launch traced here: 23.9 us
  Pallas kernels  23.2 us (96%)
  local copies, waits for them, and re-layouts  0.71 us (3%)
    pallas_call x1, Pallas kernels, gather_rows(): pl.pallas_call(functools.partial(kernel, rows, tiles, band // 2), out_sha...  23.2 us
    unnamed x1, local copies, waits for them, and re-layouts  0.71 us

profile of v4, /device:TPU:1, one launch (start us, length us, event | category | flops | bytes accessed | tf_op | source)
XLA Modules:
  0.0 23.9 jit_solution(10623339205867431300)
XLA Ops:
  0.0 23.2 %shard_map.82 = f32[2,64,512]{2,1,0:T(8,128)S(1)} custom-call(bf16[64,1024]{1,0:T(8,128)(2,1)} %bitcast.5, bf16[128,128]{1,0:T(8,128)(2,1)} %bitcast.8, bf16[14,4,16,64]{3,2,1,0:T(8,128)(2,1)} %rw_hbm.1, s32[4,7,4,16]{3,2,1,0:T(4,128)} %bitcast.6, s32[4,7,4,16]{3,2,1,0:T(4,128)} %bitcast.7, s32[4,4,4,7]{3,2,1,0:T(4,128)} %bitcast.9, f32[2,64,512]{2,1,0:T(8,128)} %vol_hbm.1, ...), custom_call_target="tpu_custom_call" | custom-call | tf_op jit(solution)/shard_map/pallas_call | solution.py:243
  23.2 0.7 %copy.10 = f32[2,64,512]{2,1,0:T(8,128)} copy(f32[2,64,512]{2,1,0:T(8,128)S(1)} %shard_map.82) | data formatting | bytes 524288
